TPU v7x, 32 devices: a whole 2x2x4 slice. The times are simulated.
32 devices in a mesh: aux: 16 (over z, y, x), orb: 2 (over core).
Axes of the slice: x: 2, y: 2, z: 4, core: 2. Of those that a mesh axis runs over, the one named last changes fastest.
Arguments:
- integrals: bfloat16 [384, 8, 4096], P('aux', 'orb'), may hold values from -6 to 6
- coefficients: bfloat16 [6144, 192], P('orb'), may hold values from -0.375 to 0.375
- metric: bfloat16 [384, 384], P('aux'), may hold values from -0.3125 to 0.3125
- mu_blocks: int32 [16, 8], P('aux', 'orb'), may hold values from 0 to 95
- nu_blocks: int32 [16, 8], P('aux', 'orb'), may hold values from 0 to 47
- counts: int32 [16, 2], P('aux', 'orb'), may hold values from 1 to 4, as said below
Outputs:
- pair_major: bfloat16 [192, 6144, 384], P('aux', 'orb')
Inputs may be any that keep to these rules, and one draw needn't show every extreme that they name: `counts`: each entry is between 1 and 4; in every draw some device holds exactly 4 live slots. `mu_blocks`: block pairs may repeat; repeated pairs add.
All inputs are finite; a program needn't handle non-finite values.
Results may differ from a plain program's by a relative error of at most 0.0049.
Values may be sent and summed in bfloat16 or wider, within the bound.
A program may use at most 192 MiB of HBM per device.

v0:
```python
import jax
import jax.numpy as jnp
from jax import lax
from jax.sharding import PartitionSpec as P

BLK = 64
NBF = 6144


def body(integrals, coefficients, metric, mu_blocks, nu_blocks, counts):
    coef_wide = lax.all_gather(coefficients, "orb", axis=0, tiled=True)
    aux_local = integrals.shape[0]
    slot_count = integrals.shape[1]
    occ_total = coef_wide.shape[1]
    nu_local = NBF // lax.axis_size("orb")
    live_count = counts[0, 0]
    partial_value = jnp.zeros((aux_local, occ_total, nu_local), jnp.float32)

    def add_pair(slot, partial_value):
        int_block = lax.dynamic_index_in_dim(integrals, slot, 1, keepdims=False)
        int_block = int_block.reshape(aux_local, BLK, BLK)
        coef_rows = lax.dynamic_slice_in_dim(coef_wide, mu_blocks[0, slot] * BLK, BLK, 0)
        product = jnp.einsum(
            "pmn,mi->pin", int_block, coef_rows, preferred_element_type=jnp.float32
        )
        live_mask = jnp.where(slot < live_count, 1.0, 0.0).astype(jnp.float32)
        offset = nu_blocks[0, slot] * BLK
        current = lax.dynamic_slice_in_dim(partial_value, offset, BLK, 2)
        return lax.dynamic_update_slice_in_dim(
            partial_value, current + live_mask * product, offset, 2
        )

    partial_value = lax.fori_loop(0, slot_count, add_pair, partial_value)
    half = partial_value.astype(jnp.bfloat16)
    regrouped = lax.all_to_all(half, "aux", split_axis=1, concat_axis=0, tiled=True)
    aux_total = regrouped.shape[0]
    occ_local = regrouped.shape[1]
    flat_half = regrouped.reshape(aux_total, occ_local * nu_local)
    result = lax.dot_general(
        flat_half,
        lax.all_gather(metric, "aux", axis=0, tiled=True),
        (((0,), (1,)), ((), ())),
        preferred_element_type=jnp.float32,
    )
    return result.astype(jnp.bfloat16).reshape(occ_local, nu_local, aux_total)


def solution(mesh):
    placed = (
        P("aux", "orb", None),
        P("orb", None),
        P("aux", None),
        P("aux", "orb"),
        P("aux", "orb"),
        P("aux", "orb"),
    )
    return jax.shard_map(
        body, mesh=mesh, in_specs=placed, out_specs=P("aux", "orb", None), check_vma=False
    )
```

profile of v0, /device:TPU:16, one launch (start us, length us, event | category | flops | bytes accessed | tf_op | source)
XLA Modules:
  0.0 910.4 jit_solution(3201010503398615229)
XLA Ops:
  6.5 2.5 copy.9
  9.0 0.0 all-gather.2.cloned.1.call-update
  9.1 1.6 copy.10
  10.6 12.0 %all-gather.2.cloned.1.call-done = bf16[6144,192]{1,0:T(8,128)(2,1)} async-done(((bf16[3072,192]{1,0:T(8,128)(2,1)}), bf16[6144,192]{1,0:T(8,128)(2,1)}) %all-gather.2.cloned.1.call-update) | async-done | bytes 2359312 | tf_op jit(solution)/shard_map/all_gather | solution.py:11
  22.7 23.6 %broadcast_in_dim.3 = f32[24,192,3072]{1,2,0:T(8,128)} broadcast(f32[]{:T(128)} %constant.61.clone.1), dimensions={} | broadcast | bytes 56623108 | tf_op jit(solution)/shard_map/broadcast_in_dim | solution.py:17
  46.3 39.8 %while.13 = (s32[]{:T(128)}, f32[24,192,3072]{1,2,0:T(8,128)}, s32[1,4]{1,0:T(1,128)S(1)}, s32[]{:T(128)}, s32[1,4]{1,0:T(1,128)S(1)}, /*index=5*/bf16[6144,192]...) while((s32[]{:T(128)}, f32[24,192,3072]{1,2,0:T(8,128)}, ...), condition=%wide.region_1.2_spmd, body=%wide.region_0.1_spmd.sunk | while | flops 38338568 | bytes 7307515 | solution.py:33
  46.3 0.7 fusion.16
  49.1 0.4 reshape.24
  49.4 0.2 copy.15
  49.7 1.1 fusion.17
  53.4 2.8 fusion.18
  56.2 0.7 fusion.16
  59.0 0.4 reshape.24
  59.4 0.2 copy.15
  59.6 1.1 fusion.17
  63.3 2.9 fusion.18
  66.2 0.7 fusion.16
  68.9 0.4 reshape.24
  69.3 0.2 copy.15
  69.6 1.1 fusion.17
  73.3 2.9 fusion.18
  76.1 0.7 fusion.16
  78.9 0.4 reshape.24
  79.3 0.2 copy.15
  79.5 1.1 fusion.17
  83.2 2.9 fusion.18
  86.1 59.9 %copy.11 = bf16[24,192,3072]{2,0,1:T(8,128)(2,1)} copy(f32[24,192,3072]{1,2,0:T(8,128)} %get-tuple-element.129) | data formatting | bytes 84934656 | tf_op jit(solution)/shard_map/while | solution.py:33
  146.0 7.1 all-to-all-start
  153.1 667.0 %all_gather.7 = bf16[384,384]{1,0:T(8,128)(2,1)S(1)} all-gather(bf16[24,384]{1,0:T(8,128)(2,1)S(1)} %copy-done), channel_id=1, replica_groups=mesh['aux'=16,'orb'=2] {'aux'}, dimensions={0}, use_global_device_ids=true | all-gather | bytes 313344 | tf_op jit(solution)/shard_map/all_gather | solution.py:41
  820.1 29.6 %copy.12 = bf16[16,24,12,3072]{3,2,1,0:T(8,128)(2,1)} copy(bf16[16,24,12,3072]{3,1,2,0:T(8,128)(2,1)} %bitcast.8) | data formatting | bytes 56623104 | tf_op jit(solution)/shard_map/all_to_all | solution.py:35
  849.7 27.1 %copy.13 = bf16[48,8,12,3072]{3,1,2,0:T(8,128)(2,1)} copy(bf16[48,8,12,3072]{3,2,1,0:T(8,128)(2,1)} %bitcast.36) | data formatting | bytes 56623104
  876.8 26.7 %convolution_convert_fusion = bf16[36864,384]{1,0:T(8,128)(2,1)} fusion(bf16[384,36864]{1,0:T(8,128)(2,1)} %bitcast.37, bf16[384,384]{1,0:T(8,128)(2,1)S(1)} %all_gather.7), kind=kOutput, calls=%fused_computation.8 | convolution fusion | flops 10885791744 | bytes 56918016 | tf_op jit(solution)/shard_map/dot_general | solution.py:39
  (12 shorter events, 0.1 us)
Async XLA Ops:
  6.5 16.1 %all-gather.2.cloned.1.call-start = ((), (), s32[]{:S(2)}) async-start(), calls=%async_computation.1 | async-start | bytes 4718592 | tf_op jit(solution)/shard_map/all_gather | solution.py:11
  22.7 23.6 %copy-start.1 = (s32[1,4]{1,0:T(1,128)S(1)}, s32[1,4]{1,0:T(1,128)}, u32[]{:S(2)}) copy-start(s32[1,4]{1,0:T(1,128)} %param.12) | copy-start | bytes 52
  22.7 23.6 %copy-start.2 = (s32[1,4]{1,0:T(1,128)S(1)}, s32[1,4]{1,0:T(1,128)}, u32[]{:S(2)}) copy-start(s32[1,4]{1,0:T(1,128)} %param.11) | copy-start | bytes 52
  146.0 7.1 copy-start
  146.0 674.1 %all-to-all-start = ((bf16[24,192,3072]{2,0,1:T(8,128)(2,1)}), bf16[24,192,3072]{2,0,1:T(8,128)(2,1)}, u32[]{:S(2)}, u32[]{:S(2)}) async-start(bf16[24,192,3072]{2,0,1:T(8,128)(2,1)} %copy.11), calls=%async_computation | async-start | bytes 56623104 | tf_op jit(solution)/shard_map/all_to_all | solution.py:35
Sparse Core Ops, SparseCore 0:
  9.2 13.4 all-gather.1
where the time goes:
time: 912 us; the launch traced here: 910 us
  blocking collectives  667 us (73%)
  local copies, waits for them, and re-layouts  147 us (16%)
  matrix products  31.1 us (3%)
  loops' own time  18.8 us (2%)
  other arithmetic  14.1 us (2%)
  between operations  13.4 us (1%)
  waiting for transfers between devices  12.1 us (1%)
    all_gather x1, blocking collectives, body(): lax.all_gather(metric, 'aux', axis=0, tiled=True)  667 us
    while x2, local copies, waits for them, and re-layouts, body(): partial_value = lax.fori_loop(0, slot_count, add_pair, partial_value)  61.5 us
    unnamed x8, local copies, waits for them, and re-layouts  29.7 us
    all_to_all x1, local copies, waits for them, and re-layouts, body(): lax.all_to_all(half, 'aux', split_axis=1, concat_axis=0, tiled=True)  29.6 us
    dot_general x1, matrix products, body(): lax.dot_general(flat_half, lax.all_gather(metric, 'aux', axis=0, tiled=Tr...  26.7 us
    broadcast_in_dim x1, local copies, waits for them, and re-layouts, body(): partial_value = jnp.zeros((aux_local, occ_total, nu_local), jnp.float32)  23.6 us
    another operation x1, loops' own time, body(): partial_value = lax.fori_loop(0, slot_count, add_pair, partial_value)  18.8 us
  transfers between devices with their start and end apart: 2, of which 1 were waited for; matrix products, arithmetic and copies ran while one was open for 0% of the time, Pallas kernels for 0%

commit v1 on v0

v1 whole, which is shorter than its diff:
```python
import functools

import jax
import jax.numpy as jnp
from jax import lax
from jax.experimental import pallas as pl
from jax.experimental.pallas import tpu as pltpu
from jax.sharding import PartitionSpec as P

BLK = 64
MESH = pl.DeviceIdType.MESH


def exchange_kernel(n, msg_ref, recv_ref, send_sem, recv_sem, own_sem):
    me = lax.axis_index("aux")
    orb = lax.axis_index("orb")
    barrier = pltpu.get_barrier_semaphore()
    for k in range(1, n):
        pl.semaphore_signal(
            barrier, inc=1, device_id=(lax.rem(me + k, n), orb), device_id_type=MESH
        )
    pl.semaphore_wait(barrier, n - 1)
    order = sorted(range(1, n), key=lambda k: abs(k - n // 2))
    copies = []
    for k in order:
        peer = lax.rem(me + k, n)
        copy = pltpu.make_async_remote_copy(
            src_ref=msg_ref.at[peer],
            dst_ref=recv_ref.at[me],
            send_sem=send_sem.at[k],
            recv_sem=recv_sem.at[k],
            device_id=(peer, orb),
            device_id_type=MESH,
        )
        copy.start()
        copies.append((k, copy))
    own = pltpu.make_async_copy(msg_ref.at[me], recv_ref.at[me], own_sem)
    own.start()
    own.wait()
    for k, copy in copies:
        copy.wait_send()
        source = lax.rem(me - k + n, n)
        pltpu.make_async_remote_copy(
            src_ref=msg_ref.at[source],
            dst_ref=recv_ref.at[source],
            send_sem=send_sem.at[k],
            recv_sem=recv_sem.at[k],
            device_id=(source, orb),
            device_id_type=MESH,
        ).wait_recv()


def exchange(msg, n):
    return pl.pallas_call(
        functools.partial(exchange_kernel, n),
        out_shape=jax.ShapeDtypeStruct(msg.shape, msg.dtype),
        in_specs=[pl.BlockSpec(memory_space=pl.ANY)],
        out_specs=pl.BlockSpec(memory_space=pl.ANY),
        scratch_shapes=[
            pltpu.SemaphoreType.DMA((n,)),
            pltpu.SemaphoreType.DMA((n,)),
            pltpu.SemaphoreType.DMA,
        ],
        compiler_params=pltpu.CompilerParams(collective_id=0, has_side_effects=True),
        name="exchange_slots",
    )(msg)


def contract_kernel(
    n_aux, slots, aux_dev, pad, occ_local, nu_blk, levels,
    nu_ref, recv_ref, met_ref, out_ref,
    padded, lhs, wgt, obuf, zero, sems, count, lists,
):
    total = n_aux * slots
    lanes = occ_local * BLK
    aux_total = out_ref.shape[2]

    def clear(b, _):
        count[b] = 0
        return 0

    lax.fori_loop(0, nu_blk, clear, 0)

    def enlist(e, _):
        b = nu_ref[e]

        @pl.when(b >= 0)
        def _():
            c = count[b]
            lists[b * n_aux + c] = e
            count[b] = c + 1

        return 0

    lax.fori_loop(0, total, enlist, 0)

    zero[...] = jnp.zeros_like(zero)
    padded[total] = jnp.zeros((pad, lanes), padded.dtype)

    def spread(a, _):
        rows = recv_ref[a]
        for s in range(slots):
            part = rows[s * aux_dev : (s + 1) * aux_dev]
            padded[a * slots + s] = jnp.concatenate(
                [part, jnp.zeros((pad - aux_dev, lanes), part.dtype)], axis=0
            )
        return 0

    lax.fori_loop(0, n_aux, spread, 0)

    def out_copy(src, b, which):
        return pltpu.make_async_copy(
            src, out_ref.at[:, pl.ds(pl.multiple_of(b * BLK, BLK), BLK), :], sems.at[which]
        )

    nbuf = obuf.shape[0]

    def block(b, _):
        which = lax.rem(b, nbuf)
        c = count[b]

        @pl.when(b >= nbuf)
        def _():
            out_copy(zero, b - nbuf, which).wait()

        @pl.when(c == 0)
        def _():
            out_copy(zero, b, which).start()

        low = 0
        for level in levels:

            @pl.when((c > low) & (c <= level))
            def _(level=level):
                for j in range(level):
                    e = jnp.where(j < c, lists[b * n_aux + jnp.minimum(j, c - 1)], total)
                    a = jnp.where(j < c, e // slots, 0)
                    lhs[j * pad : (j + 1) * pad, :] = padded[e]
                    wgt[j * pad : (j + 1) * pad, :] = met_ref[a]
                depth = level * pad
                step = 128 if lanes % 128 == 0 else lanes
                for at in range(0, lanes, step):
                    res = lax.dot_general(
                        lhs[:depth, at : at + step],
                        wgt[:depth, :],
                        (((0,), (0,)), ((), ())),
                        preferred_element_type=jnp.float32,
                    )
                    obuf[which, at // BLK : (at + step) // BLK] = res.astype(
                        obuf.dtype
                    ).reshape(step // BLK, BLK, aux_total)
                out_copy(obuf.at[which], b, which).start()

            low = level
        return 0

    lax.fori_loop(0, nu_blk, block, 0)
    for b in range(max(0, nu_blk - nbuf), nu_blk):
        out_copy(zero, b, b % nbuf).wait()


def contract(nu_lists, recv, met, occ_local, nu_local):
    n_aux, rows, lanes = recv.shape
    slots = nu_lists.shape[0] // n_aux
    aux_dev = rows // slots
    pad = met.shape[1]
    aux_total = met.shape[2]
    nu_blk = nu_local // BLK
    levels = [v for v in (2, 4, 8, 16, 32, 64) if v < n_aux] + [n_aux]
    nbuf = 4 if nu_blk >= 4 else nu_blk
    return pl.pallas_call(
        functools.partial(
            contract_kernel, n_aux, slots, aux_dev, pad, occ_local, nu_blk, levels
        ),
        out_shape=jax.ShapeDtypeStruct((occ_local, nu_local, aux_total), jnp.bfloat16),
        in_specs=[
            pl.BlockSpec(memory_space=pltpu.SMEM),
            pl.BlockSpec(memory_space=pltpu.VMEM),
            pl.BlockSpec(memory_space=pltpu.VMEM),
        ],
        out_specs=pl.BlockSpec(memory_space=pl.ANY),
        scratch_shapes=[
            pltpu.VMEM((n_aux * slots + 1, pad, lanes), jnp.bfloat16),
            pltpu.VMEM((n_aux * pad, lanes), jnp.bfloat16),
            pltpu.VMEM((n_aux * pad, aux_total), jnp.bfloat16),
            pltpu.VMEM((nbuf, occ_local, BLK, aux_total), jnp.bfloat16),
            pltpu.VMEM((occ_local, BLK, aux_total), jnp.bfloat16),
            pltpu.SemaphoreType.DMA((nbuf,)),
            pltpu.SMEM((nu_blk,), jnp.int32),
            pltpu.SMEM((nu_blk * n_aux,), jnp.int32),
        ],
        compiler_params=pltpu.CompilerParams(vmem_limit_bytes=40 * 1024 * 1024),
        name="contract_metric",
    )(nu_lists, recv, met)


def body(integrals, coefficients, metric, mu_blocks, nu_blocks, counts):
    n_aux = lax.axis_size("aux")
    aux_local, slots, _ = integrals.shape
    nbf = coefficients.shape[0] * lax.axis_size("orb")
    nu_local = nbf // lax.axis_size("orb")
    occ_total = coefficients.shape[1]
    occ_local = occ_total // n_aux
    aux_total = metric.shape[1]
    pad = -(-aux_local // 32) * 32

    nu = nu_blocks[0]
    live = jnp.arange(slots) < counts[0, 0]
    same = (nu[:, None] == nu[None, :]) & live[:, None] & live[None, :]
    first = live & ~jnp.any(jnp.tril(same, -1), axis=1)
    keep = same & first[:, None]
    nu_list = jnp.where(first, nu, -1)

    tail = jnp.zeros((pad - aux_local, aux_total), metric.dtype)
    tail = tail.at[0, :slots].set(nu_list.astype(metric.dtype))
    wide = lax.all_gather(jnp.concatenate([metric, tail], axis=0), "aux", axis=0)
    nu_lists = wide[:, aux_local, :slots].astype(jnp.int32).reshape(-1)
    met = wide[:, :aux_local].reshape(n_aux * aux_local, aux_total).T
    met = met.reshape(n_aux, aux_local, aux_total)
    met = jnp.pad(met, ((0, 0), (0, pad - aux_local), (0, 0)))

    coef_wide = lax.all_gather(coefficients, "orb", axis=0, tiled=True)
    rows = [
        lax.dynamic_slice_in_dim(coef_wide, mu_blocks[0, s] * BLK, BLK, 0)
        for s in range(slots)
    ]
    rows = jnp.stack(rows)
    coef = jnp.where(keep[:, :, None, None], rows[None], jnp.zeros_like(rows[None]))
    coef = coef.transpose(0, 3, 1, 2).reshape(slots * occ_total, slots * BLK)
    blocks = integrals.reshape(aux_local, slots, BLK, BLK).transpose(1, 2, 0, 3)
    half = jnp.dot(
        coef,
        blocks.reshape(slots * BLK, aux_local * BLK),
        preferred_element_type=jnp.float32,
    ).astype(jnp.bfloat16)
    half = half.reshape(slots, n_aux, occ_local, aux_local, BLK)
    msg = half.transpose(1, 0, 3, 2, 4).reshape(n_aux, slots * aux_local, occ_local * BLK)

    recv = exchange(msg, n_aux)
    return contract(nu_lists, recv, met, occ_local, nu_local)


def solution(mesh):
    placed = (
        P("aux", "orb", None),
        P("orb", None),
        P("aux", None),
        P("aux", "orb"),
        P("aux", "orb"),
        P("aux", "orb"),
    )
    return jax.shard_map(
        body, mesh=mesh, in_specs=placed, out_specs=P("aux", "orb", None), check_vma=False
    )
```

time: 912 us -> 161 us (0.18)
  blocking collectives: 667 us -> 32.7 us
  local copies, waits for them, and re-layouts: 147 us -> 30.9 us
  Pallas kernels: 0 us -> 78.5 us
  matrix products: 31.1 us -> 1.79 us
  loops' own time: 18.8 us -> 0 us
  other arithmetic: 14.1 us -> 0.57 us
  waiting for transfers between devices: 12.1 us -> 0.02 us
    all_gather x1, blocking collectives: 667 us -> 32.7 us  [body(): lax.all_gather(jnp.concatenate([metric, tail], axis=0), 'aux', axis=0)]
    pallas_call x0 -> x2, Pallas kernels: none -> 78.5 us  [the longest x1 60.1 us: exchange(): pl.pallas_call(functools.partial(exchange_kernel, n), out_shape=jax.Shape...]
    while x2 -> x0, local copies, waits for them, and re-layouts: 61.5 us -> none  [body(): partial_value = lax.fori_loop(0, slot_count, add_pair, partial_value)]
    all_to_all x1 -> x0, local copies, waits for them, and re-layouts: 29.6 us -> none  [body(): lax.all_to_all(half, 'aux', split_axis=1, concat_axis=0, tiled=True)]
    unnamed x8 -> x13, local copies, waits for them, and re-layouts: 29.7 us -> 4.26 us
    dot_general x1, matrix products: 26.7 us -> 1.79 us  [body(): jnp.dot(coef, blocks.reshape(slots * BLK, aux_local * BLK), preferred_ele...]
    broadcast_in_dim x1 -> x0, local copies, waits for them, and re-layouts: 23.6 us -> none  [body(): partial_value = jnp.zeros((aux_local, occ_total, nu_local), jnp.float32)]
    reshape x8 -> x6, local copies, waits for them, and re-layouts: 2.4 us -> 23 us  [the longest x2 11.4 us: body(): half = half.reshape(slots, n_aux, occ_local, aux_local, BLK)]
  transfers between devices with their start and end apart: 2 -> 1, of which waited for: 1 -> 0; matrix products, arithmetic and copies ran while one was open for 0% -> 3% of each run, Pallas kernels for 0% -> 0%
where the time goes in v1:
time: 161 us
  Pallas kernels  78.5 us (49%)
  blocking collectives  32.7 us (20%)
  local copies, waits for them, and re-layouts  30.9 us (19%)
  between operations  16.7 us (10%)
  matrix products  1.79 us (1%)
    pallas_call x1, Pallas kernels, exchange(): pl.pallas_call(functools.partial(exchange_kernel, n), out_shape=jax.Shape...  60.1 us
    all_gather x1, blocking collectives, body(): lax.all_gather(jnp.concatenate([metric, tail], axis=0), 'aux', axis=0)  32.7 us
    pallas_call x1, Pallas kernels, contract(): pl.pallas_call(functools.partial(contract_kernel, n_aux, slots, aux_dev,...  18.4 us
    reshape x2, local copies, waits for them, and re-layouts, body(): half = half.reshape(slots, n_aux, occ_local, aux_local, BLK)  11.4 us
    reshape x1, local copies, waits for them, and re-layouts, body(): half.transpose(1, 0, 3, 2, 4)  8.36 us
    unnamed x13, local copies, waits for them, and re-layouts  4.26 us
  transfers between devices with their start and end apart: 1, of which 0 were waited for; matrix products, arithmetic and copies ran while one was open for 3% of the time, Pallas kernels for 0%

profile of v1, /device:TPU:16, one launch (start us, length us, event | category | flops | bytes accessed | tf_op | source)
XLA Modules:
  0.0 161.2 jit_solution(4291972256659251401)
XLA Ops:
  6.5 0.0 copy-start.5
  6.5 0.0 copy-start.3
  6.5 0.0 copy-start.2
  6.5 0.0 all-gather.3.cloned.1.call-start
  6.6 2.6 %copy.10 = bf16[3072,192]{1,0:T(8,128)(2,1)} copy(bf16[3072,192]{0,1:T(8,128)(2,1)} %param.9) | data formatting | bytes 2359296 | tf_op args[1]
  9.2 0.0 all-gather.3.cloned.1.call-update
  9.2 0.0 copy-done.5
  9.2 0.6 fusion.7
  12.9 0.0 copy-done.4
  12.9 0.1 fusion.4
  13.0 0.0 copy-done.3
  13.1 32.7 %all-gather = bf16[512,384]{1,0:T(8,128)(2,1)S(1)} all-gather(bf16[32,384]{1,0:T(8,128)(2,1)S(1)} %fusion.1), channel_id=2, replica_groups=mesh['aux'=16,'orb'=2] {'aux'}, dimensions={0}, use_global_device_ids=true | all-gather | bytes 417792 | tf_op jit(solution)/shard_map/all_gather | solution.py:216
  45.8 0.1 reshape.181.nu_ref
  45.9 0.9 copy.13
  46.8 0.0 copy-done.2
  46.8 1.2 reshape.175
  48.1 1.0 copy.17
  49.1 0.0 copy-start.1
  49.1 1.0 reshape.176
  50.1 0.0 copy-done.1
  50.2 0.1 broadcast_and_fusion
  50.3 0.8 dynamic-slice_bitcast_fusion.3
  51.1 0.3 broadcast_select_fusion
  51.4 1.2 select_n.43
  52.6 1.8 %convolution_convert_fusion = bf16[768,1536]{1,0:T(8,128)(2,1)S(1)} fusion(bf16[768,256]{0,1:T(8,128)(2,1)} %select_n.43, bf16[256,1536]{1,0:T(8,128)(2,1)S(1)} %reshape.176), kind=kOutput, calls=%fused_computation.1 | convolution fusion | flops 605159424 | bytes 3538944 | tf_op jit(solution)/shard_map/dot_general | solution.py:231
  54.4 4.5 %reshape.177 = bf16[4,16,12,24,64]{4,3,2,1,0:T(8,128)(2,1)} reshape(bf16[768,1536]{1,0:T(8,128)(2,1)S(1)} %convolution_convert_fusion) | data formatting | bytes 4718592 | tf_op jit(solution)/shard_map/reshape | solution.py:236
  58.9 6.9 %copy.16 = bf16[4,16,12,24,64]{4,2,3,0,1:T(8,128)(2,1)} copy(bf16[4,16,12,24,64]{4,3,2,1,0:T(8,128)(2,1)} %reshape.177) | data formatting | bytes 4718592 | tf_op jit(solution)/shard_map/reshape | solution.py:236
  65.8 8.4 %reshape.178.msg_ref = bf16[16,96,768]{2,1,0:T(8,128)(2,1)} reshape(bf16[16,4,24,12,64]{4,3,2,1,0:T(8,128)(2,1)} %bitcast.42) | data formatting | bytes 4718592 | tf_op jit(solution)/shard_map/reshape | solution.py:237
  74.2 60.1 %exchange_slots.1.recv_ref = bf16[16,96,768]{2,1,0:T(8,128)(2,1)} custom-call(bf16[16,96,768]{2,1,0:T(8,128)(2,1)} %reshape.178.msg_ref), custom_call_target="tpu_custom_call" | custom-call | tf_op jit(solution)/shard_map/exchange_slots/pallas_call | solution.py:54
  134.3 0.0 copy-start
  134.3 1.7 %copy-done = bf16[16,96,768]{2,1,0:T(8,128)(2,1)S(1)} copy-done((bf16[16,96,768]{2,1,0:T(8,128)(2,1)S(1)}, bf16[16,96,768]{2,1,0:T(8,128)(2,1)}, u32[]{:S(2)}) %copy-start) | copy-done | bytes 2359320
  136.0 18.4 %contract_metric.1 = bf16[12,3072,384]{2,1,0:T(8,128)(2,1)} custom-call(s32[64]{0:T(128)S(1)} %reshape.181.nu_ref, bf16[16,96,768]{2,1,0:T(8,128)(2,1)S(1)} %copy-done, bf16[16,32,384]{2,1,0:T(8,128)(2,1)S(1)} %pad.9.met_ref), custom_call_target="tpu_custom_call" | custom-call | tf_op jit(solution)/shard_map/contract_metric/pallas_call | solution.py:171
  (11 shorter events, 0.2 us)
Async XLA Ops:
  6.5 2.7 %copy-start.5 = (s32[1,4]{1,0:T(1,128)S(1)}, s32[1,4]{1,0:T(1,128)}, u32[]{:S(2)}) copy-start(s32[1,4]{1,0:T(1,128)} %param.11) | copy-start | bytes 52
  6.5 6.4 %copy-start.4 = (s32[1,4]{1,0:T(1,128)S(1)}, s32[1,4]{1,0:T(1,128)}, u32[]{:S(2)}) copy-start(s32[1,4]{1,0:T(1,128)} %param.12) | copy-start | bytes 52
  6.5 6.5 %copy-start.3 = (bf16[24,384]{1,0:T(8,128)(2,1)S(1)}, bf16[24,384]{1,0:T(8,128)(2,1)}, u32[]{:S(2)}) copy-start(bf16[24,384]{1,0:T(8,128)(2,1)} %param.10) | copy-start | bytes 55300
  6.5 40.3 %copy-start.2 = (bf16[24,4,4096]{2,1,0:T(4,128)(2,1)S(1)}, bf16[24,4,4096]{2,1,0:T(4,128)(2,1)}, u32[]{:S(2)}) copy-start(bf16[24,4,4096]{2,1,0:T(4,128)(2,1)} %param.8) | copy-start | bytes 2359300
  6.5 43.7 %all-gather.3.cloned.1.call-start = ((), (), s32[]{:S(2)}) async-start(), calls=%async_computation | async-start | bytes 4718592 | tf_op jit(solution)/shard_map/all_gather | solution.py:222
  49.1 1.0 copy-start.1
  134.3 1.7 %copy-start = (bf16[16,96,768]{2,1,0:T(8,128)(2,1)S(1)}, bf16[16,96,768]{2,1,0:T(8,128)(2,1)}, u32[]{:S(2)}) copy-start(bf16[16,96,768]{2,1,0:T(8,128)(2,1)} %exchange_slots.1.recv_ref) | copy-start | bytes 7077892
Sparse Core Ops, SparseCore 0:
  9.3 13.4 all-gather.2

commit v2 on v1

v2 whole, which is shorter than its diff:
```python
import functools

import jax
import jax.numpy as jnp
from jax import lax
from jax.experimental import pallas as pl
from jax.experimental.pallas import tpu as pltpu
from jax.sharding import PartitionSpec as P

BLK = 64
MESH = pl.DeviceIdType.MESH


def mate_kernel(mine_ref, both_ref, send_sem, recv_sem, own_sem):
    aux = lax.axis_index("aux")
    orb = lax.axis_index("orb")
    barrier = pltpu.get_barrier_semaphore()
    pl.semaphore_signal(barrier, inc=1, device_id=(aux, 1 - orb), device_id_type=MESH)
    pl.semaphore_wait(barrier, 1)
    copy = pltpu.make_async_remote_copy(
        src_ref=mine_ref,
        dst_ref=both_ref.at[orb],
        send_sem=send_sem,
        recv_sem=recv_sem,
        device_id=(aux, 1 - orb),
        device_id_type=MESH,
    )
    copy.start()
    own = pltpu.make_async_copy(mine_ref, both_ref.at[orb], own_sem)
    own.start()
    own.wait()
    copy.wait_send()
    pltpu.make_async_remote_copy(
        src_ref=mine_ref,
        dst_ref=both_ref.at[1 - orb],
        send_sem=send_sem,
        recv_sem=recv_sem,
        device_id=(aux, 1 - orb),
        device_id_type=MESH,
    ).wait_recv()


def gather_coefficients(coefficients):
    if lax.axis_size("orb") != 2:
        return lax.all_gather(coefficients, "orb", axis=0, tiled=True)
    both = pl.pallas_call(
        mate_kernel,
        out_shape=jax.ShapeDtypeStruct((2,) + coefficients.shape, coefficients.dtype),
        in_specs=[pl.BlockSpec(memory_space=pl.ANY)],
        out_specs=pl.BlockSpec(memory_space=pl.ANY),
        scratch_shapes=[pltpu.SemaphoreType.DMA] * 3,
        compiler_params=pltpu.CompilerParams(collective_id=1, has_side_effects=True),
        name="mate_coefficients",
    )(coefficients)
    return both.reshape(-1, coefficients.shape[1])


def half_kernel(aux_dev, slots, n_aux, high, coef_ref, blocks_ref, msg_ref, rows_ref):
    def one(p, _):
        x = blocks_ref[p]
        z = jnp.zeros_like(x)
        wide = jnp.concatenate(
            [jnp.concatenate([x, z], axis=1), jnp.concatenate([z, x], axis=1)], axis=0
        )
        part = jnp.dot(coef_ref[...], wide, preferred_element_type=jnp.float32)
        rows_ref[pl.ds(p, part.shape[0], stride=aux_dev), :] = part
        return 0

    lax.fori_loop(0, aux_dev, one, 0, unroll=2)

    def pack(d, _):
        for i in range(high):
            parts = []
            for s in range(slots):
                at = ((s * n_aux + d) * high + i) * aux_dev
                parts.append(rows_ref[pl.ds(pl.multiple_of(at, 8), aux_dev), :])
            msg_ref[d, :, i * 128 : (i + 1) * 128] = jnp.concatenate(parts, axis=0).astype(
                msg_ref.dtype
            )
        return 0

    lax.fori_loop(0, n_aux, pack, 0)


def half_messages(coef, blocks, n_aux, slots, high):
    aux_dev = blocks.shape[0]
    return pl.pallas_call(
        functools.partial(half_kernel, aux_dev, slots, n_aux, high),
        out_shape=jax.ShapeDtypeStruct((n_aux, slots * aux_dev, high * 128), jnp.bfloat16),
        in_specs=[pl.BlockSpec(memory_space=pltpu.VMEM)] * 2,
        out_specs=pl.BlockSpec(memory_space=pltpu.VMEM),
        scratch_shapes=[pltpu.VMEM((coef.shape[0] * aux_dev, 128), jnp.float32)],
        compiler_params=pltpu.CompilerParams(vmem_limit_bytes=40 * 1024 * 1024),
        name="half_messages",
    )(coef, blocks)


def exchange_kernel(
    n, share, msg_ref, meta_ref, recv_ref, *rest
):
    metas_ref, mates_ref = rest[0], (rest[1] if share == 2 else None)
    send_sem, recv_sem, msend_sem, mrecv_sem, own_sem = rest[share:]
    me = lax.axis_index("aux")
    orb = lax.axis_index("orb")
    barrier = pltpu.get_barrier_semaphore()
    for k in range(1, n):
        pl.semaphore_signal(
            barrier, inc=1, device_id=(lax.rem(me + k, n), orb), device_id_type=MESH
        )
    if share == 2:
        pl.semaphore_signal(barrier, inc=1, device_id=(me, 1 - orb), device_id_type=MESH)
    pl.semaphore_wait(barrier, n - 1 + (share == 2))
    order = sorted(range(1, n), key=lambda k: abs(k - n // 2))

    def meta_copy(k, peer, slab):
        return pltpu.make_async_remote_copy(
            src_ref=meta_ref,
            dst_ref=metas_ref.at[slab],
            send_sem=msend_sem.at[k],
            recv_sem=mrecv_sem.at[k],
            device_id=(peer, orb),
            device_id_type=MESH,
        )

    def msg_copy(k, peer, slab):
        return pltpu.make_async_remote_copy(
            src_ref=msg_ref.at[peer],
            dst_ref=recv_ref.at[slab],
            send_sem=send_sem.at[k],
            recv_sem=recv_sem.at[k],
            device_id=(peer, orb),
            device_id_type=MESH,
        )

    for k in order:
        meta_copy(k, lax.rem(me + k, n), me).start()
    for k in order:
        msg_copy(k, lax.rem(me + k, n), me).start()
    own = pltpu.make_async_copy(msg_ref.at[me], recv_ref.at[me], own_sem.at[0])
    own.start()
    own_meta = pltpu.make_async_copy(meta_ref, metas_ref.at[me], own_sem.at[1])
    own_meta.start()
    own_meta.wait()
    for k in order:
        source = lax.rem(me - k + n, n)
        meta_copy(k, source, source).wait_recv()
    if share == 2:
        hand = pltpu.make_async_remote_copy(
            src_ref=metas_ref,
            dst_ref=mates_ref,
            send_sem=msend_sem.at[0],
            recv_sem=mrecv_sem.at[0],
            device_id=(me, 1 - orb),
            device_id_type=MESH,
        )
        hand.start()
        hand.wait()
    own.wait()
    for k in order:
        peer = lax.rem(me + k, n)
        source = lax.rem(me - k + n, n)
        meta_copy(k, peer, me).wait_send()
        msg_copy(k, peer, me).wait_send()
        msg_copy(k, source, source).wait_recv()


def exchange(msg, meta, n, share):
    metas = jax.ShapeDtypeStruct((n,) + meta.shape, meta.dtype)
    return pl.pallas_call(
        functools.partial(exchange_kernel, n, share),
        out_shape=[jax.ShapeDtypeStruct(msg.shape, msg.dtype)] + [metas] * share,
        in_specs=[pl.BlockSpec(memory_space=pl.ANY)] * 2,
        out_specs=[pl.BlockSpec(memory_space=pl.ANY)] * (1 + share),
        scratch_shapes=[pltpu.SemaphoreType.DMA((n,))] * 4 + [pltpu.SemaphoreType.DMA((2,))],
        compiler_params=pltpu.CompilerParams(collective_id=0, has_side_effects=True),
        name="exchange_slots",
    )(msg, meta)


def contract_kernel(
    n_aux, slots, aux_dev, pad, occ_local, nu_blk, levels,
    nu_ref, recv_ref, met_ref, out_ref,
    held, padded, lhs, wgt, obuf, zero, sems, zsems, lsem, count, lists,
):
    total = n_aux * slots
    lanes = occ_local * BLK
    aux_total = out_ref.shape[2]

    def clear(b, _):
        count[b] = 0
        return 0

    lax.fori_loop(0, nu_blk, clear, 0)

    def enlist(e, _):
        b = nu_ref[e]

        @pl.when(b >= 0)
        def _():
            c = count[b]
            lists[b * n_aux + c] = e
            count[b] = c + 1

        return 0

    lax.fori_loop(0, total, enlist, 0)

    def out_copy(src, b, sem):
        return pltpu.make_async_copy(
            src, out_ref.at[:, pl.ds(pl.multiple_of(b * BLK, BLK), BLK), :], sem
        )

    load = pltpu.make_async_copy(recv_ref, held, lsem)
    load.start()
    zero[...] = jnp.zeros_like(zero)

    def empty(b, _):
        @pl.when(count[b] == 0)
        def _():
            out_copy(zero, b, zsems.at[b]).start()

        return 0

    lax.fori_loop(0, nu_blk, empty, 0)
    padded[total] = jnp.zeros((pad, lanes), padded.dtype)
    load.wait()

    def spread(a, _):
        rows = held[a]
        for s in range(slots):
            part = rows[s * aux_dev : (s + 1) * aux_dev]
            padded[a * slots + s] = jnp.concatenate(
                [part, jnp.zeros((pad - aux_dev, lanes), part.dtype)], axis=0
            )
        return 0

    lax.fori_loop(0, n_aux, spread, 0)
    nbuf = obuf.shape[0]
    high = occ_local // 2

    def block(b, used):
        c = count[b]
        which = lax.rem(used, nbuf)

        @pl.when((c > 0) & (used >= nbuf))
        def _():
            out_copy(obuf.at[which], b, sems.at[which]).wait()

        low = 0
        for level in levels:

            @pl.when((c > low) & (c <= level))
            def _(level=level):
                for j in range(level):
                    e = jnp.where(j < c, lists[b * n_aux + jnp.minimum(j, c - 1)], total)
                    a = jnp.where(j < c, e // slots, 0)
                    lhs[j * pad : (j + 1) * pad, :] = padded[e]
                    wgt[j * pad : (j + 1) * pad, :] = met_ref[a]
                depth = level * pad
                for i in range(high):
                    res = lax.dot_general(
                        lhs[:depth, i * 128 : (i + 1) * 128],
                        wgt[:depth, :],
                        (((0,), (0,)), ((), ())),
                        preferred_element_type=jnp.float32,
                    ).astype(obuf.dtype)
                    obuf[which, i] = res[:BLK]
                    obuf[which, i + high] = res[BLK:]
                out_copy(obuf.at[which], b, sems.at[which]).start()

            low = level
        return jnp.where(c > 0, used + 1, used)

    used = lax.fori_loop(0, nu_blk, block, 0)
    for w in range(nbuf):

        @pl.when(used > w)
        def _():
            out_copy(obuf.at[w], 0, sems.at[w]).wait()

    def drain(b, _):
        @pl.when(count[b] == 0)
        def _():
            out_copy(zero, b, zsems.at[b]).wait()

        return 0

    lax.fori_loop(0, nu_blk, drain, 0)


def contract(nu_lists, recv, met, occ_local, nu_local):
    n_aux, rows, lanes = recv.shape
    slots = nu_lists.shape[0] // n_aux
    aux_dev = rows // slots
    pad = met.shape[1]
    aux_total = met.shape[2]
    nu_blk = nu_local // BLK
    levels = [v for v in (1, 2, 4, 8, 16, 32, 64) if v < n_aux] + [n_aux]
    nbuf = 4 if nu_blk >= 4 else nu_blk
    return pl.pallas_call(
        functools.partial(
            contract_kernel, n_aux, slots, aux_dev, pad, occ_local, nu_blk, levels
        ),
        out_shape=jax.ShapeDtypeStruct((occ_local, nu_local, aux_total), jnp.bfloat16),
        in_specs=[
            pl.BlockSpec(memory_space=pltpu.SMEM),
            pl.BlockSpec(memory_space=pl.ANY),
            pl.BlockSpec(memory_space=pltpu.VMEM),
        ],
        out_specs=pl.BlockSpec(memory_space=pl.ANY),
        scratch_shapes=[
            pltpu.VMEM(recv.shape, jnp.bfloat16),
            pltpu.VMEM((n_aux * slots + 1, pad, lanes), jnp.bfloat16),
            pltpu.VMEM((n_aux * pad, lanes), jnp.bfloat16),
            pltpu.VMEM((n_aux * pad, aux_total), jnp.bfloat16),
            pltpu.VMEM((nbuf, occ_local, BLK, aux_total), jnp.bfloat16),
            pltpu.VMEM((occ_local, BLK, aux_total), jnp.bfloat16),
            pltpu.SemaphoreType.DMA((nbuf,)),
            pltpu.SemaphoreType.DMA((nu_blk,)),
            pltpu.SemaphoreType.DMA,
            pltpu.SMEM((nu_blk,), jnp.int32),
            pltpu.SMEM((nu_blk * n_aux,), jnp.int32),
        ],
        compiler_params=pltpu.CompilerParams(vmem_limit_bytes=40 * 1024 * 1024),
        name="contract_metric",
    )(nu_lists, recv, met)


def body(integrals, coefficients, metric, mu_blocks, nu_blocks, counts):
    n_aux = lax.axis_size("aux")
    aux_local, slots, _ = integrals.shape
    nbf = coefficients.shape[0] * lax.axis_size("orb")
    nu_local = nbf // lax.axis_size("orb")
    occ_total = coefficients.shape[1]
    occ_local = occ_total // n_aux
    aux_total = metric.shape[1]
    pad = -(-aux_local // 32) * 32

    nu = nu_blocks[0]
    live = jnp.arange(slots) < counts[0, 0]
    same = (nu[:, None] == nu[None, :]) & live[:, None] & live[None, :]
    first = live & ~jnp.any(jnp.tril(same, -1), axis=1)
    keep = same & first[:, None]
    nu_list = jnp.where(first, nu, -1)

    orb = lax.axis_index("orb")
    share = 2 if lax.axis_size("orb") == 2 else 1
    part = aux_local // share
    tall = -(-(part + 1) // 16) * 16
    own_rows = lax.dynamic_slice_in_dim(metric, orb * part if share == 2 else 0, part, 0)
    tail = jnp.zeros((tall - part, aux_total), metric.dtype)
    tail = tail.at[0, :slots].set(nu_list.astype(metric.dtype))
    meta = jnp.concatenate([own_rows, tail], axis=0)

    coef_wide = gather_coefficients(coefficients)
    rows = jnp.stack(
        [
            lax.dynamic_slice_in_dim(coef_wide, mu_blocks[0, s] * BLK, BLK, 0)
            for s in range(slots)
        ]
    )
    high = occ_local // 2
    coef = rows.reshape(slots, BLK, n_aux, 2, high).transpose(2, 4, 3, 0, 1)
    coef = coef.reshape(1, n_aux * high, 2, slots, BLK)
    coef = jnp.where(keep[:, None, None, :, None], coef, jnp.zeros_like(coef))
    coef = coef.reshape(slots * n_aux * high, 2 * slots * BLK)
    blocks = integrals.reshape(aux_local, slots * BLK, BLK)
    msg = half_messages(coef, blocks, n_aux, slots, high)

    recv, *metas = exchange(msg, meta, n_aux, share)
    nu_lists = metas[0][:, part, :slots].astype(jnp.int32).reshape(-1)
    if share == 2:
        swap = orb == 1
        first_rows = jnp.where(swap, metas[1], metas[0])
        second_rows = jnp.where(swap, metas[0], metas[1])
        wide = jnp.concatenate([first_rows[:, :part], second_rows[:, :part]], axis=1)
    else:
        wide = metas[0][:, :part]
    met = wide.reshape(n_aux * aux_local, aux_total).T
    met = met.reshape(n_aux, aux_local, aux_total)
    met = jnp.pad(met, ((0, 0), (0, pad - aux_local), (0, 0)))
    return contract(nu_lists, recv, met, occ_local, nu_local)


def solution(mesh):
    placed = (
        P("aux", "orb", None),
        P("orb", None),
        P("aux", None),
        P("aux", "orb"),
        P("aux", "orb"),
        P("aux", "orb"),
    )
    return jax.shard_map(
        body, mesh=mesh, in_specs=placed, out_specs=P("aux", "orb", None), check_vma=False
    )
```

time: 161 us -> 157 us (0.975)
  Pallas kernels: 78.5 us -> 139 us
  blocking collectives: 32.7 us -> 0 us
  local copies, waits for them, and re-layouts: 30.9 us -> 9.75 us
  between operations: 16.7 us -> 3.48 us
  other arithmetic: 0.57 us -> 5.41 us
  matrix products: 1.79 us -> 0 us
    pallas_call x1 -> x3, Pallas kernels: 60.1 us -> 119 us  [the longest x1 65.3 us: exchange(): pl.pallas_call(functools.partial(exchange_kernel, n, share), out_shape=[j...]
    all_gather x1 -> x0, blocking collectives: 32.7 us -> none  [body(): lax.all_gather(jnp.concatenate([metric, tail], axis=0), 'aux', axis=0)]
    reshape x6 -> x2, local copies, waits for them, and re-layouts: 23 us -> 2.89 us  [the longest x1 2.67 us: body(): blocks = integrals.reshape(aux_local, slots * BLK, BLK)]
    dot_general x1 -> x0, matrix products: 1.79 us -> none  [body(): jnp.dot(coef, blocks.reshape(slots * BLK, aux_local * BLK), preferred_ele...]
  transfers between devices with their start and end apart: 1 -> 0, of which waited for: 0 -> 0; matrix products, arithmetic and copies ran while one was open for 3% -> 0% of each run, Pallas kernels for 0% -> 0%
where the time goes in v2:
time: 157 us
  Pallas kernels  139 us (89%)
  local copies, waits for them, and re-layouts  9.75 us (6%)
  other arithmetic  5.41 us (3%)
  between operations  3.48 us (2%)
    pallas_call x1, Pallas kernels, exchange(): pl.pallas_call(functools.partial(exchange_kernel, n, share), out_shape=[j...  65.3 us
    pallas_call x1, Pallas kernels, gather_coefficients(): pl.pallas_call(mate_kernel, out_shape=jax.ShapeDtypeStruct((2,) + coeffic...  48.8 us
    pallas_call x1, Pallas kernels, contract(): pl.pallas_call(functools.partial(contract_kernel, n_aux, slots, aux_dev,...  19.7 us
    pallas_call x1, Pallas kernels, half_messages(): pl.pallas_call(functools.partial(half_kernel, aux_dev, slots, n_aux, high...  4.82 us
    unnamed x13, local copies, waits for them, and re-layouts  3.38 us

profile of v2, /device:TPU:16, one launch (start us, length us, event | category | flops | bytes accessed | tf_op | source)
XLA Modules:
  0.0 157.2 jit_solution(3309823485059516080)
XLA Ops:
  0.0 0.0 copy-start
  0.8 0.8 fusion.3
  1.6 0.7 fusion.5
  2.3 0.8 broadcast_and_fusion
  3.1 1.5 fusion.6
  7.1 0.0 copy-done
  7.1 0.6 fusion.1.meta_ref
  7.7 2.7 %reshape.169.blocks_ref = bf16[24,256,64]{2,1,0:T(8,128)(2,1)S(1)} reshape(bf16[24,4,4096]{2,1,0:T(4,128)(2,1)} %param.8) | data formatting | bytes 1572864 | tf_op jit(solution)/shard_map/reshape | solution.py:367
  10.4 1.5 copy.16.mine_ref
  11.9 48.8 %mate_coefficients.1 = bf16[2,3072,192]{2,1,0:T(8,128)(2,1)} custom-call(bf16[3072,192]{1,0:T(8,128)(2,1)} %copy.16.mine_ref), custom_call_target="tpu_custom_call" | custom-call | tf_op jit(solution)/shard_map/mate_coefficients/pallas_call | solution.py:46
  60.7 0.9 constant_dynamic-slice_fusion.4
  61.6 0.1 copy.25
  61.7 0.1 copy.27
  61.9 0.1 copy.26
  62.0 0.1 copy.28
  62.2 0.1 maximum_bitcast_fusion
  62.3 0.2 copy.21
  62.5 0.2 copy.22
  62.6 0.3 broadcast_select_fusion
  62.9 0.4 select_n.50
  63.3 0.2 copy.23.coef_ref
  63.5 4.8 %half_messages.1.msg_ref = bf16[16,96,768]{2,1,0:T(8,128)(2,1)S(1)} custom-call(bf16[384,512]{1,0:T(8,128)(2,1)S(1)} %copy.23.coef_ref, bf16[24,256,64]{2,1,0:T(8,128)(2,1)S(1)} %reshape.169.blocks_ref), custom_call_target="tpu_custom_call" | custom-call | tf_op jit(solution)/shard_map/half_messages/pallas_call | solution.py:87
  68.3 0.0 copy-start.1
  68.4 1.4 copy-done.1
  69.7 65.3 %exchange_slots.1 = (bf16[16,96,768]{2,1,0:T(8,128)(2,1)}, bf16[16,16,384]{2,1,0:T(8,128)(2,1)}, bf16[16,16,384]{2,1,0:T(8,128)(2,1)}) custom-call(bf16[16,96,768]{2,1,0:T(8,128)(2,1)} %copy-done.1, bf16[16,384]{1,0:T(8,128)(2,1)} %fusion.1.meta_ref), custom_call_target="tpu_custom_call" | custom-call | tf_op jit(solution)/shard_map/exchange_slots/pallas_call | solution.py:169
  135.1 0.0 copy-start.2
  135.1 0.9 convert_reduce_fusion
  136.0 0.1 reshape.172.nu_ref
  136.1 1.1 broadcast_select_fusion.2
  137.2 0.1 pad_maximum_fusion
  137.3 0.2 copy.24
  137.5 19.7 %contract_metric.1 = bf16[12,3072,384]{2,1,0:T(8,128)(2,1)} custom-call(s32[64]{0:T(128)S(1)} %reshape.172.nu_ref, bf16[16,96,768]{2,1,0:T(8,128)(2,1)S(1)} %copy-done.2, bf16[16,32,384]{2,1,0:T(8,128)(2,1)S(1)} %pad.9.met_ref), custom_call_target="tpu_custom_call" | custom-call | tf_op jit(solution)/shard_map/contract_metric/pallas_call | solution.py:300
  (12 shorter events, 0.2 us)
Async XLA Ops:
  0.0 7.1 %copy-start = (bf16[24,384]{1,0:T(8,128)(2,1)S(1)}, bf16[24,384]{1,0:T(8,128)(2,1)}, u32[]{:S(2)}) copy-start(bf16[24,384]{1,0:T(8,128)(2,1)} %param.10) | copy-start | bytes 55300
  0.0 10.4 %copy-start.3 = (bf16[3072,192]{0,1:T(8,128)(2,1)S(1)}, bf16[3072,192]{0,1:T(8,128)(2,1)}, u32[]{:S(2)}) copy-start(bf16[3072,192]{0,1:T(8,128)(2,1)} %param.9) | copy-start | bytes 3538948
  68.3 1.4 copy-start.1
  135.1 2.5 %copy-start.2 = (bf16[16,96,768]{2,1,0:T(8,128)(2,1)S(1)}, bf16[16,96,768]{2,1,0:T(8,128)(2,1)}, u32[]{:S(2)}) copy-start(bf16[16,96,768]{2,1,0:T(8,128)(2,1)} %get-tuple-element.21.recv_ref) | copy-start | bytes 7077892

commit v3 on v2

--- a/solution.py
+++ b/solution.py
@@ -40,19 +40,56 @@
     ).wait_recv()
 
 
-def gather_coefficients(coefficients):
+def swap_mates(mine, collective_id, name):
+    return pl.pallas_call(
+        mate_kernel,
+        out_shape=jax.ShapeDtypeStruct((2,) + mine.shape, mine.dtype),
+        in_specs=[pl.BlockSpec(memory_space=pltpu.VMEM)],
+        out_specs=pl.BlockSpec(memory_space=pltpu.VMEM),
+        scratch_shapes=[pltpu.SemaphoreType.DMA] * 3,
+        compiler_params=pltpu.CompilerParams(
+            collective_id=collective_id, has_side_effects=True
+        ),
+        name=name,
+    )(mine)
+
+
+def arrange(rows, n_aux, high):
+    slots = rows.shape[0]
+    rows = rows.reshape(slots, BLK, n_aux, 2, high).transpose(2, 4, 3, 0, 1)
+    return rows.reshape(n_aux * high, 2 * slots * BLK)
+
+
+def listed_coefficients(coefficients, mu, n_aux, high):
+    slots = mu.shape[0]
+
+    def pick(source, at):
+        return jnp.stack(
+            [lax.dynamic_slice_in_dim(source, at[s] * BLK, BLK, 0) for s in range(slots)]
+        )
+
     if lax.axis_size("orb") != 2:
-        return lax.all_gather(coefficients, "orb", axis=0, tiled=True)
-    both = pl.pallas_call(
-        mate_kernel,
-        out_shape=jax.ShapeDtypeStruct((2,) + coefficients.shape, coefficients.dtype),
-        in_specs=[pl.BlockSpec(memory_space=pl.ANY)],
-        out_specs=pl.BlockSpec(memory_space=pl.ANY),
-        scratch_shapes=[pltpu.SemaphoreType.DMA] * 3,
-        compiler_params=pltpu.CompilerParams(collective_id=1, has_side_effects=True),
-        name="mate_coefficients",
-    )(coefficients)
-    return both.reshape(-1, coefficients.shape[1])
+        wide = lax.all_gather(coefficients, "orb", axis=0, tiled=True)
+        return arrange(pick(wide, mu), n_aux, high)
+    orb = lax.axis_index("orb")
+    held = coefficients.shape[0] // BLK
+    asked = jnp.zeros((8, 128), jnp.int32).at[0, :slots].set(mu)
+    asked = swap_mates(asked, 1, "swap_lists")[:, 0, :slots]
+    mates = jnp.where(orb == 0, asked[1], asked[0])
+
+    def from_own(at):
+        near = at - orb * held
+        return arrange(pick(coefficients, jnp.clip(near, 0, held - 1)), n_aux, high)
+
+    given = swap_mates(from_own(mates), 2, "swap_rows")
+    given = jnp.where(orb == 0, given[1], given[0])
+    mine = from_own(mu)
+    near = mu // held == orb
+    shape = (n_aux * high, 2, slots, BLK)
+    merged = jnp.where(
+        near[None, None, :, None], mine.reshape(shape), given.reshape(shape)
+    )
+    return merged.reshape(mine.shape)
 
 
 def half_kernel(aux_dev, slots, n_aux, high, coef_ref, blocks_ref, msg_ref, rows_ref):
@@ -352,15 +389,8 @@
     tail = tail.at[0, :slots].set(nu_list.astype(metric.dtype))
     meta = jnp.concatenate([own_rows, tail], axis=0)
 
-    coef_wide = gather_coefficients(coefficients)
-    rows = jnp.stack(
-        [
-            lax.dynamic_slice_in_dim(coef_wide, mu_blocks[0, s] * BLK, BLK, 0)
-            for s in range(slots)
-        ]
-    )
     high = occ_local // 2
-    coef = rows.reshape(slots, BLK, n_aux, 2, high).transpose(2, 4, 3, 0, 1)
+    coef = listed_coefficients(coefficients, mu_blocks[0], n_aux, high)
     coef = coef.reshape(1, n_aux * high, 2, slots, BLK)
     coef = jnp.where(keep[:, None, None, :, None], coef, jnp.zeros_like(coef))
     coef = coef.reshape(slots * n_aux * high, 2 * slots * BLK)

time: 157 us -> 118 us (0.75)
  Pallas kernels: 139 us -> 93.6 us
  other arithmetic: 5.41 us -> 8.69 us
  between operations: 3.48 us -> 5.79 us
    pallas_call x1 -> x2, Pallas kernels: 48.8 us -> 5.36 us  [swap_mates(): pl.pallas_call(mate_kernel, out_shape=jax.ShapeDtypeStruct((2,) + mine.sh...]
    unnamed x13 -> x8, local copies, waits for them, and re-layouts: 3.38 us -> 1.41 us
where the time goes in v3:
time: 118 us; the launch traced here: 117 us
  Pallas kernels  93.6 us (79%)
  local copies, waits for them, and re-layouts  9.07 us (8%)
  other arithmetic  8.69 us (7%)
  between operations  5.79 us (5%)
    pallas_call x1, Pallas kernels, exchange(): pl.pallas_call(functools.partial(exchange_kernel, n, share), out_shape=[j...  65.2 us
    pallas_call x1, Pallas kernels, contract(): pl.pallas_call(functools.partial(contract_kernel, n_aux, slots, aux_dev,...  18.2 us
    pallas_call x2, Pallas kernels, swap_mates(): pl.pallas_call(mate_kernel, out_shape=jax.ShapeDtypeStruct((2,) + mine.sh...  5.36 us
    pallas_call x1, Pallas kernels, half_messages(): pl.pallas_call(functools.partial(half_kernel, aux_dev, slots, n_aux, high...  4.82 us

profile of v3, /device:TPU:16, one launch (start us, length us, event | category | flops | bytes accessed | tf_op | source)
XLA Modules:
  0.0 117.1 jit_solution(1663276944269375880)
XLA Ops:
  0.7 0.7 fusion.7
  1.3 0.7 subtract_clamp_fusion
  2.0 0.8 fusion.3
  2.8 0.7 fusion.8
  3.5 0.8 broadcast_and_fusion
  4.3 0.6 fusion.9
  7.4 1.3 %scatter.6.mine_ref = s32[8,128]{1,0:T(8,128)} pad(s32[1,4]{1,0:T(1,128)} %param.13, s32[]{:T(128)} %constant.93.clone.1), padding=0_7x0_124 | pad | bytes 4116 | tf_op jit(solution)/shard_map/scatter | solution.py:76
  8.6 2.5 %swap_lists.1 = s32[2,8,128]{2,1,0:T(8,128)} custom-call(s32[8,128]{1,0:T(8,128)} %scatter.6.mine_ref), custom_call_target="tpu_custom_call" | custom-call | tf_op jit(solution)/shard_map/swap_lists/pallas_call | solution.py:44
  11.1 0.7 fusion.6
  11.8 0.6 fusion.10
  14.9 0.6 fusion.1.meta_ref
  15.5 1.2 %constant_dynamic-slice_fusion.8 = (bf16[64,192]{0,1:T(8,128)(2,1)S(1)}, bf16[64,192]{0,1:T(8,128)(2,1)S(1)}, bf16[64,192]{0,1:T(8,128)(2,1)S(1)}, bf16[64,192]{...) fusion(bf16[3072,192]{0,1:T(8,128)(2,1)} %param.11, ...), kind=kLoop, calls=%fused_computation.20 | loop fusion | bytes 393248 | tf_op jit(solution)/shard_map/dynamic_slice | solution.py:68
  17.0 0.2 copy.12
  17.3 0.2 copy.13
  17.5 0.8 reshape.304.mine_ref
  18.3 2.9 %swap_rows.1 = bf16[2,96,512]{2,1,0:T(8,128)(2,1)} custom-call(bf16[96,512]{1,0:T(8,128)(2,1)} %reshape.304.mine_ref), custom_call_target="tpu_custom_call" | custom-call | tf_op jit(solution)/shard_map/swap_rows/pallas_call | solution.py:44
  21.2 1.0 slice_select_fusion
  22.2 0.1 copy.14
  22.3 0.2 copy.15
  22.5 0.2 bitcast_select_fusion
  22.7 0.2 copy.16
  22.9 0.3 broadcast_select_fusion
  23.2 0.4 select_n.115
  23.6 0.2 copy.17.coef_ref
  23.8 1.2 %reshape.305.blocks_ref = bf16[24,256,64]{2,1,0:T(8,128)(2,1)S(1)} reshape(bf16[24,4,4096]{2,1,0:T(4,128)(2,1)S(1)} %copy-done.3) | data formatting | bytes 1572864 | tf_op jit(solution)/shard_map/reshape | solution.py:397
  25.0 4.8 %half_messages.1.msg_ref = bf16[16,96,768]{2,1,0:T(8,128)(2,1)S(1)} custom-call(bf16[384,512]{1,0:T(8,128)(2,1)S(1)} %copy.17.coef_ref, bf16[24,256,64]{2,1,0:T(8,128)(2,1)S(1)} %reshape.305.blocks_ref), custom_call_target="tpu_custom_call" | custom-call | tf_op jit(solution)/shard_map/half_messages/pallas_call | solution.py:124
  29.9 1.4 %copy-done.1 = bf16[16,96,768]{2,1,0:T(8,128)(2,1)} copy-done((bf16[16,96,768]{2,1,0:T(8,128)(2,1)}, bf16[16,96,768]{2,1,0:T(8,128)(2,1)S(1)}, u32[]{:S(2)}) %copy-start.1) | copy-done | bytes 2359320
  31.2 65.2 %exchange_slots.1 = (bf16[16,96,768]{2,1,0:T(8,128)(2,1)}, bf16[16,16,384]{2,1,0:T(8,128)(2,1)}, bf16[16,16,384]{2,1,0:T(8,128)(2,1)}) custom-call(bf16[16,96,768]{2,1,0:T(8,128)(2,1)} %copy-done.1, bf16[16,384]{1,0:T(8,128)(2,1)} %fusion.1.meta_ref), custom_call_target="tpu_custom_call" | custom-call | tf_op jit(solution)/shard_map/exchange_slots/pallas_call | solution.py:206
  96.4 0.9 convert_reduce_fusion
  97.5 1.1 broadcast_select_fusion.2
  98.6 0.2 copy.18
  98.9 18.2 %contract_metric.1 = bf16[12,3072,384]{2,1,0:T(8,128)(2,1)} custom-call(s32[64]{0:T(128)S(1)} %reshape.308.nu_ref, bf16[16,96,768]{2,1,0:T(8,128)(2,1)S(1)} %copy-done.2, bf16[16,32,384]{2,1,0:T(8,128)(2,1)S(1)} %pad.13.met_ref), custom_call_target="tpu_custom_call" | custom-call | tf_op jit(solution)/shard_map/contract_metric/pallas_call | solution.py:337
  (24 shorter events, 0.7 us)
Async XLA Ops:
  0.0 14.9 %copy-start = (bf16[24,384]{1,0:T(8,128)(2,1)S(1)}, bf16[24,384]{1,0:T(8,128)(2,1)}, u32[]{:S(2)}) copy-start(bf16[24,384]{1,0:T(8,128)(2,1)} %param.12) | copy-start | bytes 55300
  17.5 6.3 %copy-start.3 = (bf16[24,4,4096]{2,1,0:T(4,128)(2,1)S(1)}, bf16[24,4,4096]{2,1,0:T(4,128)(2,1)}, u32[]{:S(2)}) copy-start(bf16[24,4,4096]{2,1,0:T(4,128)(2,1)} %param.10) | copy-start | bytes 2359300
  29.8 1.4 %copy-start.1 = (bf16[16,96,768]{2,1,0:T(8,128)(2,1)}, bf16[16,96,768]{2,1,0:T(8,128)(2,1)S(1)}, u32[]{:S(2)}) copy-start(bf16[16,96,768]{2,1,0:T(8,128)(2,1)S(1)} %half_messages.1.msg_ref) | copy-start | bytes 7077892
  96.4 2.5 %copy-start.2 = (bf16[16,96,768]{2,1,0:T(8,128)(2,1)S(1)}, bf16[16,96,768]{2,1,0:T(8,128)(2,1)}, u32[]{:S(2)}) copy-start(bf16[16,96,768]{2,1,0:T(8,128)(2,1)} %get-tuple-element.33.recv_ref) | copy-start | bytes 7077892

commit v4 on v3

--- a/solution.py
+++ b/solution.py
@@ -73,7 +73,7 @@
         return arrange(pick(wide, mu), n_aux, high)
     orb = lax.axis_index("orb")
     held = coefficients.shape[0] // BLK
-    asked = jnp.zeros((8, 128), jnp.int32).at[0, :slots].set(mu)
+    asked = jnp.pad(mu[None], ((0, 7), (0, 128 - slots)))
     asked = swap_mates(asked, 1, "swap_lists")[:, 0, :slots]
     mates = jnp.where(orb == 0, asked[1], asked[0])
 
@@ -147,7 +147,12 @@
     if share == 2:
         pl.semaphore_signal(barrier, inc=1, device_id=(me, 1 - orb), device_id_type=MESH)
     pl.semaphore_wait(barrier, n - 1 + (share == 2))
-    order = sorted(range(1, n), key=lambda k: abs(k - n // 2))
+    by_distance = sorted(range(1, n), key=lambda k: abs(k - n // 2))
+    order = []
+    while by_distance:
+        order.append(by_distance.pop(0))
+        if by_distance:
+            order.append(by_distance.pop())
 
     def meta_copy(k, peer, slab):
         return pltpu.make_async_remote_copy(
@@ -385,8 +390,8 @@
     part = aux_local // share
     tall = -(-(part + 1) // 16) * 16
     own_rows = lax.dynamic_slice_in_dim(metric, orb * part if share == 2 else 0, part, 0)
-    tail = jnp.zeros((tall - part, aux_total), metric.dtype)
-    tail = tail.at[0, :slots].set(nu_list.astype(metric.dtype))
+    tail = nu_list.astype(metric.dtype)[None]
+    tail = jnp.pad(tail, ((0, tall - part - 1), (0, aux_total - slots)))
     meta = jnp.concatenate([own_rows, tail], axis=0)
 
     high = occ_local // 2

time: 118 us -> 115 us (0.975)
  Pallas kernels: 93.6 us -> 89.8 us
    pallas_call x1, Pallas kernels: 65.2 us -> 61.4 us  [exchange(): pl.pallas_call(functools.partial(exchange_kernel, n, share), out_shape=[j...]
    pad x0 -> x1, local copies, waits for them, and re-layouts: none -> 1.25 us  [listed_coefficients(): asked = jnp.pad(mu[None], ((0, 7), (0, 128 - slots)))]
    scatter x1 -> x0, local copies, waits for them, and re-layouts: 1.25 us -> none  [listed_coefficients(): asked = jnp.zeros((8, 128), jnp.int32).at[0, :slots].set(mu)]
where the time goes in v4:
time: 115 us; the launch traced here: 113 us
  Pallas kernels  89.8 us (78%)
  local copies, waits for them, and re-layouts  9.21 us (8%)
  other arithmetic  8.69 us (8%)
  between operations  5.79 us (5%)
    pallas_call x1, Pallas kernels, exchange(): pl.pallas_call(functools.partial(exchange_kernel, n, share), out_shape=[j...  61.4 us
    pallas_call x1, Pallas kernels, contract(): pl.pallas_call(functools.partial(contract_kernel, n_aux, slots, aux_dev,...  18.3 us
    pallas_call x2, Pallas kernels, swap_mates(): pl.pallas_call(mate_kernel, out_shape=jax.ShapeDtypeStruct((2,) + mine.sh...  5.36 us
    pallas_call x1, Pallas kernels, half_messages(): pl.pallas_call(functools.partial(half_kernel, aux_dev, slots, n_aux, high...  4.82 us

profile of v4, /device:TPU:16, one launch (start us, length us, event | category | flops | bytes accessed | tf_op | source)
XLA Modules:
  0.0 113.5 jit_solution(11271029175456190779)
XLA Ops:
  0.7 0.7 fusion.7
  1.3 0.7 subtract_clamp_fusion
  2.0 0.8 fusion.3
  2.8 0.7 fusion.8
  3.5 0.8 broadcast_and_fusion
  4.3 0.6 fusion.9
  7.4 1.3 %pad.12.mine_ref = s32[8,128]{1,0:T(8,128)} pad(s32[1,4]{1,0:T(1,128)} %param.9, s32[]{:T(128)} %constant.45.clone.1), padding=0_7x0_124 | pad | bytes 4116 | tf_op jit(solution)/shard_map/jit(_pad)/pad | solution.py:76
  8.6 2.5 %swap_lists.1 = s32[2,8,128]{2,1,0:T(8,128)} custom-call(s32[8,128]{1,0:T(8,128)} %pad.12.mine_ref), custom_call_target="tpu_custom_call" | custom-call | tf_op jit(solution)/shard_map/swap_lists/pallas_call | solution.py:44
  11.1 0.7 fusion.6
  11.8 0.6 fusion.10
  14.9 0.6 fusion.1.meta_ref
  15.5 1.3 %constant_dynamic-slice_fusion.8 = (bf16[64,192]{0,1:T(8,128)(2,1)S(1)}, bf16[64,192]{0,1:T(8,128)(2,1)S(1)}, bf16[64,192]{0,1:T(8,128)(2,1)S(1)}, bf16[64,192]{...) fusion(bf16[3072,192]{0,1:T(8,128)(2,1)} %param.7, ...), kind=kLoop, calls=%fused_computation.20 | loop fusion | bytes 393248 | tf_op jit(solution)/shard_map/dynamic_slice | solution.py:68
  17.1 0.2 copy.12
  17.5 0.2 copy.13
  17.6 0.8 reshape.254.mine_ref
  18.5 2.9 %swap_rows.1 = bf16[2,96,512]{2,1,0:T(8,128)(2,1)} custom-call(bf16[96,512]{1,0:T(8,128)(2,1)} %reshape.254.mine_ref), custom_call_target="tpu_custom_call" | custom-call | tf_op jit(solution)/shard_map/swap_rows/pallas_call | solution.py:44
  21.4 1.0 slice_select_fusion
  22.3 0.1 copy.14
  22.4 0.2 copy.15
  22.6 0.2 bitcast_select_fusion
  22.8 0.2 copy.16
  23.0 0.3 broadcast_select_fusion
  23.3 0.4 select_n.115
  23.7 0.2 copy.17.coef_ref
  23.9 1.2 %reshape.255.blocks_ref = bf16[24,256,64]{2,1,0:T(8,128)(2,1)S(1)} reshape(bf16[24,4,4096]{2,1,0:T(4,128)(2,1)S(1)} %copy-done.3) | data formatting | bytes 1572864 | tf_op jit(solution)/shard_map/reshape | solution.py:402
  25.1 4.8 %half_messages.1.msg_ref = bf16[16,96,768]{2,1,0:T(8,128)(2,1)S(1)} custom-call(bf16[384,512]{1,0:T(8,128)(2,1)S(1)} %copy.17.coef_ref, bf16[24,256,64]{2,1,0:T(8,128)(2,1)S(1)} %reshape.255.blocks_ref), custom_call_target="tpu_custom_call" | custom-call | tf_op jit(solution)/shard_map/half_messages/pallas_call | solution.py:124
  30.0 1.4 %copy-done.1 = bf16[16,96,768]{2,1,0:T(8,128)(2,1)} copy-done((bf16[16,96,768]{2,1,0:T(8,128)(2,1)}, bf16[16,96,768]{2,1,0:T(8,128)(2,1)S(1)}, u32[]{:S(2)}) %copy-start.1) | copy-done | bytes 2359320
  31.4 61.4 %exchange_slots.1 = (bf16[16,96,768]{2,1,0:T(8,128)(2,1)}, bf16[16,16,384]{2,1,0:T(8,128)(2,1)}, bf16[16,16,384]{2,1,0:T(8,128)(2,1)}) custom-call(bf16[16,96,768]{2,1,0:T(8,128)(2,1)} %copy-done.1, bf16[16,384]{1,0:T(8,128)(2,1)} %fusion.1.meta_ref), custom_call_target="tpu_custom_call" | custom-call | tf_op jit(solution)/shard_map/exchange_slots/pallas_call | solution.py:211
  92.7 0.9 convert_reduce_fusion
  93.8 1.1 broadcast_select_fusion.2
  94.9 0.2 copy.18
  95.2 18.3 %contract_metric.1 = bf16[12,3072,384]{2,1,0:T(8,128)(2,1)} custom-call(s32[64]{0:T(128)S(1)} %reshape.258.nu_ref, bf16[16,96,768]{2,1,0:T(8,128)(2,1)S(1)} %copy-done.2, bf16[16,32,384]{2,1,0:T(8,128)(2,1)S(1)} %pad.14.met_ref), custom_call_target="tpu_custom_call" | custom-call | tf_op jit(solution)/shard_map/contract_metric/pallas_call | solution.py:342
  (24 shorter events, 0.7 us)
Async XLA Ops:
  0.0 14.9 %copy-start = (bf16[24,384]{1,0:T(8,128)(2,1)S(1)}, bf16[24,384]{1,0:T(8,128)(2,1)}, u32[]{:S(2)}) copy-start(bf16[24,384]{1,0:T(8,128)(2,1)} %param.8) | copy-start | bytes 55300
  17.6 6.3 %copy-start.3 = (bf16[24,4,4096]{2,1,0:T(4,128)(2,1)S(1)}, bf16[24,4,4096]{2,1,0:T(4,128)(2,1)}, u32[]{:S(2)}) copy-start(bf16[24,4,4096]{2,1,0:T(4,128)(2,1)} %param.6) | copy-start | bytes 2359300
  30.0 1.4 %copy-start.1 = (bf16[16,96,768]{2,1,0:T(8,128)(2,1)}, bf16[16,96,768]{2,1,0:T(8,128)(2,1)S(1)}, u32[]{:S(2)}) copy-start(bf16[16,96,768]{2,1,0:T(8,128)(2,1)S(1)} %half_messages.1.msg_ref) | copy-start | bytes 7077892
  92.7 2.5 %copy-start.2 = (bf16[16,96,768]{2,1,0:T(8,128)(2,1)S(1)}, bf16[16,96,768]{2,1,0:T(8,128)(2,1)}, u32[]{:S(2)}) copy-start(bf16[16,96,768]{2,1,0:T(8,128)(2,1)} %get-tuple-element.9.recv_ref) | copy-start | bytes 7077892

commit v5 on v4

--- a/solution.py
+++ b/solution.py
@@ -103,7 +103,7 @@
         rows_ref[pl.ds(p, part.shape[0], stride=aux_dev), :] = part
         return 0
 
-    lax.fori_loop(0, aux_dev, one, 0, unroll=2)
+    lax.fori_loop(0, aux_dev, one, 0, unroll=4)
 
     def pack(d, _):
         for i in range(high):
@@ -228,6 +228,9 @@
     lanes = occ_local * BLK
     aux_total = out_ref.shape[2]
 
+    load = pltpu.make_async_copy(recv_ref, held, lsem)
+    load.start()
+
     def clear(b, _):
         count[b] = 0
         return 0
@@ -252,8 +255,6 @@
             src, out_ref.at[:, pl.ds(pl.multiple_of(b * BLK, BLK), BLK), :], sem
         )
 
-    load = pltpu.make_async_copy(recv_ref, held, lsem)
-    load.start()
     zero[...] = jnp.zeros_like(zero)
 
     def empty(b, _):
@@ -276,7 +277,7 @@
             )
         return 0
 
-    lax.fori_loop(0, n_aux, spread, 0)
+    lax.fori_loop(0, n_aux, spread, 0, unroll=2)
     nbuf = obuf.shape[0]
     high = occ_local // 2
 

time: 115 us -> 114 us (level)
  no operation moved by 1% of the time
where the time goes in v5:
time: 114 us; the launch traced here: 113 us
  Pallas kernels  89.4 us (78%)
  local copies, waits for them, and re-layouts  9.1 us (8%)
  other arithmetic  8.69 us (8%)
  between operations  5.79 us (5%)
    pallas_call x1, Pallas kernels, exchange(): pl.pallas_call(functools.partial(exchange_kernel, n, share), out_shape=[j...  61.4 us
    pallas_call x1, Pallas kernels, contract(): pl.pallas_call(functools.partial(contract_kernel, n_aux, slots, aux_dev,...  18.8 us
    pallas_call x2, Pallas kernels, swap_mates(): pl.pallas_call(mate_kernel, out_shape=jax.ShapeDtypeStruct((2,) + mine.sh...  5.36 us
    pallas_call x1, Pallas kernels, half_messages(): pl.pallas_call(functools.partial(half_kernel, aux_dev, slots, n_aux, high...  3.81 us

profile of v5, /device:TPU:16, one launch (start us, length us, event | category | flops | bytes accessed | tf_op | source)
XLA Modules:
  0.0 113.0 jit_solution(10913355182709317786)
XLA Ops:
  0.7 0.7 fusion.7
  1.3 0.7 subtract_clamp_fusion
  2.0 0.8 fusion.3
  2.8 0.7 fusion.8
  3.5 0.8 broadcast_and_fusion
  4.3 0.6 fusion.9
  7.4 1.3 %pad.12.mine_ref = s32[8,128]{1,0:T(8,128)} pad(s32[1,4]{1,0:T(1,128)} %param.9, s32[]{:T(128)} %constant.45.clone.1), padding=0_7x0_124 | pad | bytes 4116 | tf_op jit(solution)/shard_map/jit(_pad)/pad | solution.py:76
  8.6 2.5 %swap_lists.1 = s32[2,8,128]{2,1,0:T(8,128)} custom-call(s32[8,128]{1,0:T(8,128)} %pad.12.mine_ref), custom_call_target="tpu_custom_call" | custom-call | tf_op jit(solution)/shard_map/swap_lists/pallas_call | solution.py:44
  11.1 0.7 fusion.6
  11.8 0.6 fusion.10
  14.9 0.6 fusion.1.meta_ref
  15.5 1.2 %constant_dynamic-slice_fusion.8 = (bf16[64,192]{0,1:T(8,128)(2,1)S(1)}, bf16[64,192]{0,1:T(8,128)(2,1)S(1)}, bf16[64,192]{0,1:T(8,128)(2,1)S(1)}, bf16[64,192]{...) fusion(bf16[3072,192]{0,1:T(8,128)(2,1)} %param.7, ...), kind=kLoop, calls=%fused_computation.20 | loop fusion | bytes 393248 | tf_op jit(solution)/shard_map/dynamic_slice | solution.py:68
  17.0 0.2 copy.12
  17.4 0.2 copy.13
  17.5 0.8 reshape.254.mine_ref
  18.4 2.9 %swap_rows.1 = bf16[2,96,512]{2,1,0:T(8,128)(2,1)} custom-call(bf16[96,512]{1,0:T(8,128)(2,1)} %reshape.254.mine_ref), custom_call_target="tpu_custom_call" | custom-call | tf_op jit(solution)/shard_map/swap_rows/pallas_call | solution.py:44
  21.2 1.0 slice_select_fusion
  22.2 0.1 copy.14
  22.3 0.2 copy.15
  22.5 0.2 bitcast_select_fusion
  22.7 0.2 copy.16
  22.9 0.3 broadcast_select_fusion
  23.2 0.4 select_n.115
  23.6 0.2 copy.17.coef_ref
  23.8 1.2 %reshape.255.blocks_ref = bf16[24,256,64]{2,1,0:T(8,128)(2,1)S(1)} reshape(bf16[24,4,4096]{2,1,0:T(4,128)(2,1)S(1)} %copy-done.3) | data formatting | bytes 1572864 | tf_op jit(solution)/shard_map/reshape | solution.py:403
  25.0 3.8 %half_messages.1.msg_ref = bf16[16,96,768]{2,1,0:T(8,128)(2,1)S(1)} custom-call(bf16[384,512]{1,0:T(8,128)(2,1)S(1)} %copy.17.coef_ref, bf16[24,256,64]{2,1,0:T(8,128)(2,1)S(1)} %reshape.255.blocks_ref), custom_call_target="tpu_custom_call" | custom-call | tf_op jit(solution)/shard_map/half_messages/pallas_call | solution.py:124
  28.9 1.4 %copy-done.1 = bf16[16,96,768]{2,1,0:T(8,128)(2,1)} copy-done((bf16[16,96,768]{2,1,0:T(8,128)(2,1)}, bf16[16,96,768]{2,1,0:T(8,128)(2,1)S(1)}, u32[]{:S(2)}) %copy-start.1) | copy-done | bytes 2359320
  30.3 61.4 %exchange_slots.1 = (bf16[16,96,768]{2,1,0:T(8,128)(2,1)}, bf16[16,16,384]{2,1,0:T(8,128)(2,1)}, bf16[16,16,384]{2,1,0:T(8,128)(2,1)}) custom-call(bf16[16,96,768]{2,1,0:T(8,128)(2,1)} %copy-done.1, bf16[16,384]{1,0:T(8,128)(2,1)} %fusion.1.meta_ref), custom_call_target="tpu_custom_call" | custom-call | tf_op jit(solution)/shard_map/exchange_slots/pallas_call | solution.py:211
  91.7 0.9 convert_reduce_fusion
  92.7 1.1 broadcast_select_fusion.2
  93.9 0.2 copy.18
  94.2 18.8 %contract_metric.1 = bf16[12,3072,384]{2,1,0:T(8,128)(2,1)} custom-call(s32[64]{0:T(128)S(1)} %reshape.258.nu_ref, bf16[16,96,768]{2,1,0:T(8,128)(2,1)S(1)} %copy-done.2, bf16[16,32,384]{2,1,0:T(8,128)(2,1)S(1)} %pad.14.met_ref), custom_call_target="tpu_custom_call" | custom-call | tf_op jit(solution)/shard_map/contract_metric/pallas_call | solution.py:343
  (24 shorter events, 0.7 us)
Async XLA Ops:
  0.0 14.9 %copy-start = (bf16[24,384]{1,0:T(8,128)(2,1)S(1)}, bf16[24,384]{1,0:T(8,128)(2,1)}, u32[]{:S(2)}) copy-start(bf16[24,384]{1,0:T(8,128)(2,1)} %param.8) | copy-start | bytes 55300
  17.5 6.3 %copy-start.3 = (bf16[24,4,4096]{2,1,0:T(4,128)(2,1)S(1)}, bf16[24,4,4096]{2,1,0:T(4,128)(2,1)}, u32[]{:S(2)}) copy-start(bf16[24,4,4096]{2,1,0:T(4,128)(2,1)} %param.6) | copy-start | bytes 2359300
  28.8 1.4 %copy-start.1 = (bf16[16,96,768]{2,1,0:T(8,128)(2,1)}, bf16[16,96,768]{2,1,0:T(8,128)(2,1)S(1)}, u32[]{:S(2)}) copy-start(bf16[16,96,768]{2,1,0:T(8,128)(2,1)S(1)} %half_messages.1.msg_ref) | copy-start | bytes 7077892
  91.7 2.5 %copy-start.2 = (bf16[16,96,768]{2,1,0:T(8,128)(2,1)S(1)}, bf16[16,96,768]{2,1,0:T(8,128)(2,1)}, u32[]{:S(2)}) copy-start(bf16[16,96,768]{2,1,0:T(8,128)(2,1)} %get-tuple-element.9.recv_ref) | copy-start | bytes 7077892
